TPU v7x, 512 devices: a whole 4x4x16 slice. The times are simulated.
512 devices in a mesh: ctx: 32 (over y, x, core), tp: 16 (over z).
Axes of the slice: x: 4, y: 4, z: 16, core: 2. Of those that a mesh axis runs over, the one named last changes fastest.
Arguments:
- features: bfloat16 [8192, 3, 4096], P('ctx', None, 'tp'), may hold values from -6 to 6
- short_taps: float32 [3, 3, 4096], P(None, None, 'tp'), may hold values from -3.5 to 3.5
- residues: float32 [16, 256], P(None, 'tp'), may hold values from -1.5 to 1.5
- rates: float32 [16, 256], P(None, 'tp'), may hold values from 3.6621094e-05 to 0.05, as said below
- skip: float32 [4096], P('tp'), may hold values from -4 to 4
- out_weight: bfloat16 [4096, 4096], P(None, 'tp'), may hold values from -0.09375 to 0.09375
Outputs:
- mixed: bfloat16 [8192, 4096], P('ctx', 'tp')
Inputs may be any that keep to these rules, and one draw needn't show every extreme that they name: `rates`: decay rate of one mode of one filter.
All inputs are finite; a program needn't handle non-finite values.
Results may differ from a plain program's by a relative error of at most 0.0049.
Values may be sent and summed in bfloat16 or wider, within the bound.
No kernel may reach another device: no remote copies, remote signals or barrier semaphores. Data moves between devices by JAX's collectives and lax.ppermute only.
A program may use at most 128 MiB of HBM per device.

v0:
```python
import math
import jax
import jax.numpy as jnp
from jax import lax
from jax.sharding import PartitionSpec as P

SHORT = 3


def passed_along(array, axis, by):
    count = lax.axis_size(axis)
    pairs = [(i, i + by) for i in range(count) if 0 <= i + by < count]
    return lax.ppermute(array, axis, pairs)


def regroup(block):
    return lax.all_to_all(block, "ctx", split_axis=0, concat_axis=0, tiled=True)


def mixdot(form, left, right):
    return jnp.einsum(form, left, right, precision=lax.Precision.HIGHEST)


def rotate(real_part, imag_part, cosine, sine, sign):
    return (
        real_part * cosine - sign * imag_part * sine,
        imag_part * cosine + sign * real_part * sine,
    )


def phase_table(numer, denom):
    angle = 2.0 * math.pi / denom * numer.astype(jnp.float32)
    return (jnp.cos(angle), jnp.sin(angle))


def filter_spectrum(residues, rates, own, rows, ctx_count):
    twice = 2 * ctx_count
    seq_len = rows * ctx_count
    total_len = 2 * seq_len
    sub_index = jnp.arange(2, dtype=jnp.int32)[:, None]
    freq_index = jnp.arange(rows, dtype=jnp.int32)[None, :]
    wave = 2 * own + sub_index + twice * freq_index
    signed = jnp.where(wave < seq_len, wave, wave - total_len)
    theta = 2.0 * math.pi / total_len * signed.astype(jnp.float32)
    theta = theta[None, :, :, None]
    decay = rates[:, None, None, :]
    damping = jnp.exp(-decay)
    den_real = -jnp.expm1(-decay) + damping * 2.0 * jnp.sin(0.5 * theta) ** 2
    den_imag = damping * jnp.sin(theta)
    parity = (1 - 2 * sub_index).astype(jnp.float32)[None, :, :, None]
    numer = 1.0 - jnp.exp(-decay * float(seq_len)) * parity
    scaled = (
        residues[:, None, None, :]
        * jnp.sqrt(2.0 * decay)
        * numer
        / (den_real * den_real + den_imag * den_imag)
    )
    return (jnp.sum(scaled * den_real, axis=0), -jnp.sum(scaled * den_imag, axis=0))


def transform_conv(product, residues, rates, ctx_count, own):
    rows = product.shape[0]
    width = product.shape[1]
    filters = residues.shape[1]
    piece = rows // ctx_count
    twice = 2 * ctx_count
    total_len = 2 * rows * ctx_count
    dev_index = jnp.arange(ctx_count, dtype=jnp.int32)
    freq_group = jnp.arange(twice, dtype=jnp.int32)
    cos_outer, sin_outer = phase_table(freq_group[:, None] * dev_index[None, :] % twice, twice)
    local_pos = own * piece + jnp.arange(piece, dtype=jnp.int32)
    cos_twist, sin_twist = phase_table(
        freq_group[:, None] * local_pos[None, :] % total_len, total_len
    )
    cos_twist = cos_twist[:, :, None]
    sin_twist = sin_twist[:, :, None]
    row_index = jnp.arange(rows, dtype=jnp.int32)
    cos_inner, sin_inner = phase_table(row_index[:, None] * row_index[None, :] % rows, rows)
    cos_inner = cos_inner.reshape(rows, ctx_count, piece)
    sin_inner = sin_inner.reshape(rows, ctx_count, piece)
    moved = regroup(product.reshape(ctx_count, piece, width))
    spec_real = mixdot("ca,ajm->cjm", cos_outer, moved)
    spec_imag = -mixdot("ca,ajm->cjm", sin_outer, moved)
    spec_real, spec_imag = rotate(spec_real, spec_imag, cos_twist, sin_twist, -1.0)
    outgoing = jnp.concatenate([spec_real, spec_imag], -1).reshape(ctx_count, 2 * piece, 2 * width)
    arrived = regroup(outgoing).reshape(ctx_count, 2, piece, 2 * width)
    arr_real = arrived[..., :width]
    arr_imag = arrived[..., width:]
    freq_real = mixdot("usj,scjm->cum", cos_inner, arr_real) + mixdot(
        "usj,scjm->cum", sin_inner, arr_imag
    )
    freq_imag = mixdot("usj,scjm->cum", cos_inner, arr_imag) - mixdot(
        "usj,scjm->cum", sin_inner, arr_real
    )
    filt_real, filt_imag = filter_spectrum(residues, rates, own, rows, ctx_count)
    filt_real = filt_real[..., None]
    filt_imag = filt_imag[..., None]
    freq_real = freq_real.reshape(2, rows, filters, width // filters)
    freq_imag = freq_imag.reshape(2, rows, filters, width // filters)
    prod_real = (freq_real * filt_real - freq_imag * filt_imag).reshape(2, rows, width)
    prod_imag = (freq_real * filt_imag + freq_imag * filt_real).reshape(2, rows, width)
    back_real = mixdot("usj,cum->scjm", cos_inner, prod_real) - mixdot(
        "usj,cum->scjm", sin_inner, prod_imag
    )
    back_imag = mixdot("usj,cum->scjm", sin_inner, prod_real) + mixdot(
        "usj,cum->scjm", cos_inner, prod_imag
    )
    returning = jnp.concatenate([back_real, back_imag], -1).reshape(ctx_count, 2 * piece, 2 * width)
    returned = regroup(returning).reshape(twice, piece, 2 * width)
    ret_real, ret_imag = rotate(
        returned[..., :width], returned[..., width:], cos_twist, sin_twist, 1.0
    )
    scale = 1.0 / total_len
    out_real = mixdot("ca,cjm->ajm", cos_outer, ret_real) - mixdot(
        "ca,cjm->ajm", sin_outer, ret_imag
    )
    time_rows = out_real * scale
    conv = regroup(time_rows).reshape(rows, width)
    return conv


def shards(features, short_taps, residues, rates, skip, out_weight):
    ctx_count = lax.axis_size("ctx")
    own = lax.axis_index("ctx")
    rows = features.shape[0]
    rim = passed_along(features[rows - (SHORT - 1) :], "ctx", 1)
    extended = jnp.concatenate([rim, features], 0)
    shorted = jnp.zeros(features.shape, jnp.float32)
    for shift in range(SHORT):
        window = extended[SHORT - 1 - shift : SHORT - 1 - shift + rows].astype(jnp.float32)
        shorted = shorted + short_taps[shift] * window
    query = shorted[:, 0, :]
    product = shorted[:, 1, :] * shorted[:, 2, :]
    conv = transform_conv(product, residues, rates, ctx_count, own)
    gated = (query * (conv + skip * product)).astype(jnp.bfloat16)
    projected = jnp.dot(
        lax.all_gather(gated, "tp", axis=1, tiled=True),
        out_weight,
        preferred_element_type=jnp.float32,
    )
    return projected.astype(jnp.bfloat16)


def solution(mesh):
    in_specs = (
        P("ctx", None, "tp"),
        P(None, None, "tp"),
        P(None, "tp"),
        P(None, "tp"),
        P("tp"),
        P(None, "tp"),
    )
    out_specs = P("ctx", "tp")
    return jax.shard_map(shards, mesh=mesh, in_specs=in_specs, out_specs=out_specs, check_vma=False)
```

profile of v0, /device:TPU:32, one launch (start us, length us, event | category | flops | bytes accessed | tf_op | source)
XLA Modules:
  0.0 198.4 jit_solution(7042605041022296858)
XLA Ops:
  6.5 0.9 slice.41
  7.4 1.7 collective-permute-start
  9.1 0.7 slice_bitcast_fusion.3
  9.9 1.8 multiply_add_fusion
  11.7 0.7 fusion.68
  12.5 9.7 %all-to-all-start = ((f32[32,8,256]{2,1,0:T(8,128)}), f32[32,8,256]{2,1,0:T(8,128)S(1)}, u32[]{:S(2)}, u32[]{:S(2)}) async-start(f32[32,8,256]{2,1,0:T(8,128)} %fusion.68), calls=%async_computation | async-start | bytes 524288 | tf_op jit(solution)/shard_map/all_to_all | solution.py:17
  22.3 8.8 %all-to-all-done = f32[32,8,256]{2,1,0:T(8,128)S(1)} async-done(((f32[32,8,256]{2,1,0:T(8,128)}), f32[32,8,256]{2,1,0:T(8,128)S(1)}, u32[]{:S(2)}, u32[]{:S(2)}) %all-to-all-start) | async-done | bytes 262176 | tf_op jit(solution)/shard_map/all_to_all | solution.py:17
  31.1 0.7 fusion.56
  31.8 0.8 multiply_subtract_fusion
  32.8 1.6 copy.36
  34.4 4.7 %all-to-all-start.1 = ((f32[32,16,512]{2,1,0:T(8,128)}), f32[32,16,512]{2,1,0:T(8,128)}, u32[]{:S(2)}, u32[]{:S(2)}) async-start(f32[32,16,512]{2,1,0:T(8,128)} %bitcast.118), calls=%async_computation.1 | async-start | bytes 2097152 | tf_op jit(solution)/shard_map/all_to_all | solution.py:17
  39.1 0.2 all-gather.2.cloned.1.call-start
  39.6 0.3 multiply_reduce_fusion
  39.9 16.5 %all-to-all-done.1 = f32[32,16,512]{2,1,0:T(8,128)} async-done(((f32[32,16,512]{2,1,0:T(8,128)}), f32[32,16,512]{2,1,0:T(8,128)}, u32[]{:S(2)}, u32[]{:S(2)}) %all-to-all-start.1) | async-done | bytes 1048608 | tf_op jit(solution)/shard_map/all_to_all | solution.py:17
  56.4 1.8 copy.37
  58.2 1.9 convolution_bitcast_fusion.2
  60.1 1.9 convolution_bitcast_fusion
  62.0 1.9 fusion.3
  63.9 1.9 fusion.11
  65.9 1.6 fusion.14
  67.5 1.8 fusion.16
  69.3 1.6 fusion
  70.9 1.6 fusion.1
  72.6 0.6 copy.42
  73.2 20.6 %all_to_all.20 = f32[32,16,512]{2,1,0:T(8,128)S(1)} all-to-all(f32[32,16,512]{2,1,0:T(8,128)S(1)} %copy.42), channel_id=1, replica_groups=mesh['ctx'=32,'tp'=16] {'ctx'}, dimensions={0} | all-to-all | bytes 2097152 | tf_op jit(solution)/shard_map/all_to_all | solution.py:17
  94.0 0.8 fusion.21
  94.7 0.8 fusion.6
  95.5 0.2 copy.45
  95.7 12.3 %all_to_all.21 = f32[32,8,256]{2,1,0:T(8,128)S(1)} all-to-all(f32[32,8,256]{2,1,0:T(8,128)S(1)} %copy.45), channel_id=1, replica_groups=mesh['ctx'=32,'tp'=16] {'ctx'}, dimensions={0} | all-to-all | bytes 524288 | tf_op jit(solution)/shard_map/all_to_all | solution.py:17
  107.9 0.7 fusion.38
  108.7 79.9 %all-gather.2.cloned.1.call-done = bf16[256,4096]{1,0:T(8,128)(2,1)} async-done(((bf16[256,256]{1,0:T(8,128)(2,1)}), bf16[256,4096]{1,0:T(8,128)(2,1)}) %all-gather.2.cloned.1.call-update) | async-done | bytes 2097168 | tf_op jit(solution)/shard_map/all_gather | solution.py:137
  188.6 3.0 %convolution_convert_fusion = bf16[256,256]{1,0:T(8,128)(2,1)} fusion(bf16[256,4096]{1,0:T(8,128)(2,1)} %all-gather.2.cloned.1.call-done, bf16[4096,256]{1,0:T(8,128)(2,1)S(1)} %copy-done), kind=kOutput, calls=%fused_computation.15 | convolution fusion | flops 536936448 | bytes 4325376 | tf_op jit(solution)/shard_map/dot_general | solution.py:136
  (23 shorter events, 0.8 us)
Async XLA Ops:
  6.5 182.0 %copy-start = (bf16[4096,256]{1,0:T(8,128)(2,1)S(1)}, bf16[4096,256]{1,0:T(8,128)(2,1)}, u32[]{:S(2)}) copy-start(bf16[4096,256]{1,0:T(8,128)(2,1)} %param.11) | copy-start | bytes 6291460
  7.4 2.5 %collective-permute-start = (bf16[2,3,256]{2,0,1:T(2,128)(2,1)S(1)}, bf16[2,3,256]{2,0,1:T(2,128)(2,1)S(1)}, u32[]{:S(2)}, u32[]{:S(2)}) collective-permute-start(bf16[2,3,256]{2,0,1:T(2,128)(2,1)S(1)} %slice.41), channel_id=1, source_target_pairs={{0,16},{16,32},{32,48},{48,64},{64,80},{80,96},{96,112},{112,128},... | collective-permute-start | bytes 9224 | tf_op jit(solution)/shard_map/ppermute | solution.py:13
  12.5 18.6 %all-to-all-start = ((f32[32,8,256]{2,1,0:T(8,128)}), f32[32,8,256]{2,1,0:T(8,128)S(1)}, u32[]{:S(2)}, u32[]{:S(2)}) async-start(f32[32,8,256]{2,1,0:T(8,128)} %fusion.68), calls=%async_computation | async-start | bytes 524288 | tf_op jit(solution)/shard_map/all_to_all | solution.py:17
  32.8 6.7 %copy-start.1 = (f32[16,16]{1,0:T(8,128)S(1)}, f32[16,16]{1,0:T(8,128)}, u32[]{:S(2)}) copy-start(f32[16,16]{1,0:T(8,128)} %param.8) | copy-start | bytes 3076
  32.8 6.7 %copy-start.2 = (f32[16,16]{1,0:T(8,128)S(1)}, f32[16,16]{1,0:T(8,128)}, u32[]{:S(2)}) copy-start(f32[16,16]{1,0:T(8,128)} %param.9) | copy-start | bytes 3076
  34.4 22.0 %all-to-all-start.1 = ((f32[32,16,512]{2,1,0:T(8,128)}), f32[32,16,512]{2,1,0:T(8,128)}, u32[]{:S(2)}, u32[]{:S(2)}) async-start(f32[32,16,512]{2,1,0:T(8,128)} %bitcast.118), calls=%async_computation.1 | async-start | bytes 2097152 | tf_op jit(solution)/shard_map/all_to_all | solution.py:17
  39.1 149.5 %all-gather.2.cloned.1.call-start = ((), (), s32[]{:S(2)}) async-start(), calls=%async_computation.4 | async-start | bytes 2228224 | tf_op jit(solution)/shard_map/all_gather | solution.py:137
  94.0 14.0 %copy-start.3 = (f32[256]{0:T(256)S(1)}, f32[256]{0:T(256)}, u32[]{:S(2)}) copy-start(f32[256]{0:T(256)} %param.10) | copy-start | bytes 3076
Sparse Core Ops, SparseCore 0:
  108.8 79.7 all-gather.1
where the time goes:
time: 199 us; the launch traced here: 198 us
  waiting for transfers between devices  105 us (53%)
  blocking collectives  32.9 us (17%)
  matrix products  20.2 us (10%)
  starting transfers between devices  16.3 us (8%)
  between operations  13.7 us (7%)
  local copies, waits for them, and re-layouts  5.9 us (3%)
  other arithmetic  4.2 us (2%)
    all_gather x1, waiting for transfers between devices, shards(): lax.all_gather(gated, 'tp', axis=1, tiled=True)  79.9 us
    all_to_all x2, blocking collectives, regroup(): return lax.all_to_all(block, 'ctx', split_axis=0, concat_axis=0, tiled=True)  32.9 us
    all_to_all x2, waiting for transfers between devices, regroup(): return lax.all_to_all(block, 'ctx', split_axis=0, concat_axis=0, tiled=True)  25.2 us
    dot_general x12, matrix products, mixdot(): return jnp.einsum(form, left, right, precision=lax.Precision.HIGHEST)  17.2 us
    all_to_all x2, starting transfers between devices, regroup(): return lax.all_to_all(block, 'ctx', split_axis=0, concat_axis=0, tiled=True)  14.4 us
  transfers between devices with their start and end apart: 4, of which 4 were waited for; matrix products, arithmetic and copies ran while one was open for 1% of the time, Pallas kernels for 0%

commit v1 on v0

--- a/solution.py
+++ b/solution.py
@@ -134,7 +134,9 @@
     conv = transform_conv(product, residues, rates, ctx_count, own)
     gated = (query * (conv + skip * product)).astype(jnp.bfloat16)
     projected = jnp.dot(
-        lax.all_gather(gated, "tp", axis=1, tiled=True),
+        jnp.concatenate(
+            lax.all_to_all(jnp.stack([gated] * lax.axis_size("tp")), "tp", 0, 0), axis=1
+        ),
         out_weight,
         preferred_element_type=jnp.float32,
     )

time: 199 us -> 216 us (1.085)
  blocking collectives: 32.9 us -> 145 us
  waiting for transfers between devices: 105 us -> 25.4 us
  between operations: 13.7 us -> 0.28 us
    all_to_all x0 -> x1, blocking collectives: none -> 112 us  [shards(): lax.all_to_all(jnp.stack([gated] * lax.axis_size('tp')), 'tp', 0, 0)]
    all_gather x1 -> x0, waiting for transfers between devices: 79.9 us -> none  [shards(): lax.all_gather(gated, 'tp', axis=1, tiled=True)]
  transfers between devices with their start and end apart: 4 -> 3, of which waited for: 4 -> 3; matrix products, arithmetic and copies ran while one was open for 1% -> 1% of each run, Pallas kernels for 0% -> 0%
where the time goes in v1:
time: 216 us; the launch traced here: 215 us
  blocking collectives  145 us (67%)
  waiting for transfers between devices  25.4 us (12%)
  matrix products  18.6 us (9%)
  starting transfers between devices  16.3 us (8%)
  local copies, waits for them, and re-layouts  6.2 us (3%)
  other arithmetic  3.53 us (2%)
    all_to_all x1, blocking collectives, shards(): lax.all_to_all(jnp.stack([gated] * lax.axis_size('tp')), 'tp', 0, 0)  112 us
    all_to_all x2, blocking collectives, regroup(): return lax.all_to_all(block, 'ctx', split_axis=0, concat_axis=0, tiled=True)  32.9 us
    all_to_all x2, waiting for transfers between devices, regroup(): return lax.all_to_all(block, 'ctx', split_axis=0, concat_axis=0, tiled=True)  25.3 us
    dot_general x12, matrix products, mixdot(): return jnp.einsum(form, left, right, precision=lax.Precision.HIGHEST)  17.2 us
    all_to_all x2, starting transfers between devices, regroup(): return lax.all_to_all(block, 'ctx', split_axis=0, concat_axis=0, tiled=True)  14.5 us
  transfers between devices with their start and end apart: 3, of which 3 were waited for; matrix products, arithmetic and copies ran while one was open for 1% of the time, Pallas kernels for 0%

profile of v1, /device:TPU:32, one launch (start us, length us, event | category | flops | bytes accessed | tf_op | source)
XLA Modules:
  0.0 215.3 jit_solution(5684108391675253431)
XLA Ops:
  0.0 0.9 slice.41
  0.9 1.7 collective-permute-start
  2.6 0.7 slice_bitcast_fusion.3
  3.4 1.8 multiply_add_fusion
  5.2 0.7 fusion.68
  6.0 9.7 %all-to-all-start = ((f32[32,8,256]{2,1,0:T(8,128)}), f32[32,8,256]{2,1,0:T(8,128)S(1)}, u32[]{:S(2)}, u32[]{:S(2)}) async-start(f32[32,8,256]{2,1,0:T(8,128)} %fusion.68), calls=%async_computation | async-start | bytes 524288 | tf_op jit(solution)/shard_map/all_to_all | solution.py:17
  15.8 8.8 %all-to-all-done = f32[32,8,256]{2,1,0:T(8,128)S(1)} async-done(((f32[32,8,256]{2,1,0:T(8,128)}), f32[32,8,256]{2,1,0:T(8,128)S(1)}, u32[]{:S(2)}, u32[]{:S(2)}) %all-to-all-start) | async-done | bytes 262176 | tf_op jit(solution)/shard_map/all_to_all | solution.py:17
  24.5 0.7 fusion.56
  25.3 0.8 multiply_subtract_fusion
  26.2 1.6 copy.38
  27.9 4.8 %all-to-all-start.1 = ((f32[32,16,512]{2,1,0:T(8,128)}), f32[32,16,512]{2,1,0:T(8,128)}, u32[]{:S(2)}, u32[]{:S(2)}) async-start(f32[32,16,512]{2,1,0:T(8,128)} %bitcast.121), calls=%async_computation.1 | async-start | bytes 2097152 | tf_op jit(solution)/shard_map/all_to_all | solution.py:17
  32.7 0.1 sine_multiply_fusion
  33.0 0.3 multiply_reduce_fusion
  33.3 16.5 %all-to-all-done.1 = f32[32,16,512]{2,1,0:T(8,128)} async-done(((f32[32,16,512]{2,1,0:T(8,128)}), f32[32,16,512]{2,1,0:T(8,128)}, u32[]{:S(2)}, u32[]{:S(2)}) %all-to-all-start.1) | async-done | bytes 1048608 | tf_op jit(solution)/shard_map/all_to_all | solution.py:17
  49.8 1.8 copy.39
  51.7 1.9 convolution_bitcast_fusion
  53.6 1.9 convolution_bitcast_fusion.2
  55.5 1.9 fusion.3
  57.4 1.9 fusion.11
  59.3 1.6 fusion.14
  60.9 1.8 fusion.16
  62.7 1.6 fusion.1
  64.3 1.6 fusion
  66.1 0.6 copy.44
  66.7 20.6 %all_to_all.25 = f32[32,16,512]{2,1,0:T(8,128)S(1)} all-to-all(f32[32,16,512]{2,1,0:T(8,128)S(1)} %copy.44), channel_id=1, replica_groups=mesh['ctx'=32,'tp'=16] {'ctx'}, dimensions={0} | all-to-all | bytes 2097152 | tf_op jit(solution)/shard_map/all_to_all | solution.py:17
  87.4 0.7 fusion.21
  88.2 0.8 fusion.6
  88.9 0.2 copy.47
  89.1 12.3 %all_to_all.26 = f32[32,8,256]{2,1,0:T(8,128)S(1)} all-to-all(f32[32,8,256]{2,1,0:T(8,128)S(1)} %copy.47), channel_id=1, replica_groups=mesh['ctx'=32,'tp'=16] {'ctx'}, dimensions={0} | all-to-all | bytes 524288 | tf_op jit(solution)/shard_map/all_to_all | solution.py:17
  101.5 0.2 stack.2
  101.8 112.1 %all_to_all.27 = bf16[16,256,256]{1,2,0:T(8,128)(2,1)S(1)} all-to-all(bf16[16,256,256]{1,2,0:T(8,128)(2,1)S(1)} %stack.2), channel_id=1, replica_groups=mesh['ctx'=32,'tp'=16] {'tp'}, dimensions={0} | all-to-all | bytes 4194304 | tf_op jit(solution)/shard_map/all_to_all | solution.py:138
  213.9 1.4 convolution_convert_fusion
  (23 shorter events, 0.8 us)
Async XLA Ops:
  0.0 213.9 %copy-start = (bf16[4096,256]{1,0:T(8,128)(2,1)S(1)}, bf16[4096,256]{1,0:T(8,128)(2,1)}, u32[]{:S(2)}) copy-start(bf16[4096,256]{1,0:T(8,128)(2,1)} %param.11) | copy-start | bytes 6291460
  0.9 2.5 %collective-permute-start = (bf16[2,3,256]{2,0,1:T(2,128)(2,1)S(1)}, bf16[2,3,256]{2,0,1:T(2,128)(2,1)S(1)}, u32[]{:S(2)}, u32[]{:S(2)}) collective-permute-start(bf16[2,3,256]{2,0,1:T(2,128)(2,1)S(1)} %slice.41), channel_id=1, source_target_pairs={{0,16},{16,32},{32,48},{48,64},{64,80},{80,96},{96,112},{112,128},... | collective-permute-start | bytes 9224 | tf_op jit(solution)/shard_map/ppermute | solution.py:13
  6.0 18.6 %all-to-all-start = ((f32[32,8,256]{2,1,0:T(8,128)}), f32[32,8,256]{2,1,0:T(8,128)S(1)}, u32[]{:S(2)}, u32[]{:S(2)}) async-start(f32[32,8,256]{2,1,0:T(8,128)} %fusion.68), calls=%async_computation | async-start | bytes 524288 | tf_op jit(solution)/shard_map/all_to_all | solution.py:17
  26.2 6.6 %copy-start.1 = (f32[16,16]{1,0:T(8,128)S(1)}, f32[16,16]{1,0:T(8,128)}, u32[]{:S(2)}) copy-start(f32[16,16]{1,0:T(8,128)} %param.8) | copy-start | bytes 3076
  26.2 6.6 %copy-start.2 = (f32[16,16]{1,0:T(8,128)S(1)}, f32[16,16]{1,0:T(8,128)}, u32[]{:S(2)}) copy-start(f32[16,16]{1,0:T(8,128)} %param.9) | copy-start | bytes 3076
  27.9 22.0 %all-to-all-start.1 = ((f32[32,16,512]{2,1,0:T(8,128)}), f32[32,16,512]{2,1,0:T(8,128)}, u32[]{:S(2)}, u32[]{:S(2)}) async-start(f32[32,16,512]{2,1,0:T(8,128)} %bitcast.121), calls=%async_computation.1 | async-start | bytes 2097152 | tf_op jit(solution)/shard_map/all_to_all | solution.py:17
  87.4 14.0 %copy-start.3 = (f32[256]{0:T(256)S(1)}, f32[256]{0:T(256)}, u32[]{:S(2)}) copy-start(f32[256]{0:T(256)} %param.10) | copy-start | bytes 3076
